TPU v7x, 32 devices: a whole 2x2x4 slice. The times are simulated.
32 devices in a mesh: row: 2 (over core), col: 4 (over y, x), depth: 4 (over z).
Axes of the slice: x: 2, y: 2, z: 4, core: 2. Of those that a mesh axis runs over, the one named last changes fastest.
Arguments:
- blocks: float32 [512, 4, 4, 128, 128], P(('row', 'depth'), 'col'), may hold values from -0.9 to 0.9
- columns: int32 [512, 4, 4], P(('row', 'depth'), 'col'), may hold values from 0 to 127, as said below
- counts: int32 [512, 4], P(('row', 'depth'), 'col'), may hold values from 0 to 4, as said below
Outputs:
- purified: float32 [8, 4, 4, 128, 128], P(('row', 'depth'), 'col')
Inputs may be any that keep to these rules, and one draw needn't show every extreme that they name: `columns`: the first counts[i, p] slots of block row i in panel p name distinct places; the panel that holds block column i names it in slot 0. `counts`: the panel that holds block column i has a count of 1 or more.
All inputs are finite; a program needn't handle non-finite values.
Results may differ from a plain program's by a relative error of at most 0.0003.
Values sent between devices are 32-bit elements; how exact they have to be, the bound alone decides.
A program may use at most 128 MiB of HBM per device.

v0:
```python
import functools

import jax
import jax.numpy as jnp
from jax import lax
from jax.experimental import pallas as pl
from jax.experimental.pallas import tpu as pltpu
from jax.sharding import PartitionSpec as P

MESH = pl.DeviceIdType.MESH
LANES = 128
VMEM_LIMIT = 48 << 20
TIERS = ((2, 6), (4, 8))
HEAD = 2
SOURCE = LANES // 2


def position():
    return lax.axis_index("row"), lax.axis_index("col"), lax.axis_index("depth")


def spread(cols, slots, src_ref, dst_ref, send, recv):
    r, c, d = position()

    def remote(src, dst, send, recv, column):
        return pltpu.make_async_remote_copy(
            src_ref=src, dst_ref=dst, send_sem=send, recv_sem=recv,
            device_id=(r, column, d), device_id_type=MESH,
        )

    if cols != 4 or slots % 2:
        def copy(slot, other):
            return remote(src_ref, dst_ref.at[slot], send.at[0, other], recv.at[0, slot], other)

        def begin():
            @pl.loop(1, cols)
            def _(off):
                copy(c, (c + off) % cols).start()

        def end():
            @pl.loop(1, cols)
            def _(off):
                other = (c + off) % cols
                copy(other, other).wait_recv()
                copy(c, other).wait_send()

        return begin, lambda: None, end

    def half(ref, h):
        return ref.at[:, pl.ds(h * (slots // 2), slots // 2)]

    def direct(h, way):
        return remote(
            half(src_ref, h), half(dst_ref.at[c], h), send.at[h, way - 1], recv.at[h, c], c ^ way
        )

    def arrival(h, way):
        there = half(dst_ref.at[c ^ way], h)
        return remote(half(src_ref, h), there, send.at[h, 0], recv.at[h, c ^ way], c ^ 1)

    def onward(h):
        origin = c ^ (1 + h)
        there = half(dst_ref.at[origin], h)
        return remote(there, there, send.at[h, 2], recv.at[h, origin], c ^ (2 - h))

    sent = [(0, 1), (1, 2), (1, 1), (0, 2)]

    def begin():
        for h, way in sent:
            direct(h, way).start()

    def pass_on():
        for h in (0, 1):
            arrival(h, 1 + h).wait_recv()
            onward(h).start()

    def end():
        for h, way in ((1, 1), (0, 2), (0, 3), (1, 3)):
            arrival(h, way).wait_recv()
        for h, way in sent:
            direct(h, way).wait_send()
        for h in (0, 1):
            onward(h).wait_send()

    return begin, pass_on, end


def meta_kernel(
    sizes, panels, entries, local_ref, all_ref, sibling_ref, meta_ref,
    send_sem, recv_sem, own_sem, swap_sems,
):
    rows, cols, depths = sizes
    window = rows * depths
    r, c, d = position()
    me_q = r * depths + d
    owner = d // panels
    lanes = lax.broadcasted_iota(jnp.int32, meta_ref.shape, 1)
    meta = jnp.zeros(meta_ref.shape, jnp.int32)
    for j in range(entries):
        value = jnp.broadcast_to(local_ref[j : j + 1, 0:1], meta_ref.shape)
        meta = jnp.where(lanes == j, value, meta)
    meta_ref[...] = meta

    def column_mate(off):
        q = (me_q + off) % window
        return q, c

    def inner_mate(i):
        col = (c + 1 + i // (rows * panels)) % cols
        row = (i // panels) % rows
        return row * depths + c * panels + i % panels, col

    def left_source(i):
        return i, owner

    mates = window - 1
    inner = rows * panels * (cols - 1)
    sources = jnp.where(owner == c, 0, window)

    def device(q, col):
        return (q // depths, col, q % depths)

    barrier = pltpu.get_barrier_semaphore()

    def greet(q, col):
        pl.semaphore_signal(barrier, inc=1, device_id=device(q, col), device_id_type=MESH)

    @pl.loop(1, window)
    def _(off):
        greet(*column_mate(off))

    @pl.loop(0, sources)
    def _(i):
        greet(*left_source(i))

    own = pltpu.make_async_copy(meta_ref, all_ref.at[me_q * cols + c], own_sem)
    own.start()
    pl.semaphore_wait(barrier, mates + inner)

    def copy(slot, q, col):
        return pltpu.make_async_remote_copy(
            src_ref=meta_ref,
            dst_ref=all_ref.at[slot],
            send_sem=send_sem.at[q * cols + col],
            recv_sem=recv_sem.at[slot],
            device_id=device(q, col),
            device_id_type=MESH,
        )

    me = me_q * cols + c
    swap = pltpu.make_async_remote_copy(
        src_ref=local_ref,
        dst_ref=sibling_ref,
        send_sem=swap_sems.at[0],
        recv_sem=swap_sems.at[1],
        device_id=(1 - r, c, d),
        device_id_type=MESH,
    )

    @pl.loop(0, inner)
    def _(i):
        copy(me, *inner_mate(i)).start()

    @pl.loop(1, window)
    def _(off):
        copy(me, *column_mate(off)).start()

    swap.start()
    own.wait()

    @pl.loop(1, window)
    def _(off):
        q, col = column_mate(off)
        copy(q * cols + col, q, col).wait_recv()
        copy(me, q, col).wait_send()

    @pl.loop(0, sources)
    def _(i):
        q, col = left_source(i)
        copy(q * cols + col, q, col).wait_recv()

    @pl.loop(0, inner)
    def _(i):
        copy(me, *inner_mate(i)).wait_send()

    swap.wait()


def gather_meta(local, sizes, panels, entries):
    devices = sizes[0] * sizes[1] * sizes[2]
    return pl.pallas_call(
        functools.partial(meta_kernel, sizes, panels, entries),
        out_shape=(
            jax.ShapeDtypeStruct((devices, 1, LANES), jnp.int32),
            jax.ShapeDtypeStruct(local.shape, jnp.int32),
        ),
        in_specs=[pl.BlockSpec(memory_space=pltpu.VMEM)],
        out_specs=(pl.BlockSpec(memory_space=pltpu.VMEM),) * 2,
        scratch_shapes=[
            pltpu.VMEM((1, LANES), jnp.int32),
            pltpu.SemaphoreType.DMA((devices,)),
            pltpu.SemaphoreType.DMA((devices,)),
            pltpu.SemaphoreType.DMA,
            pltpu.SemaphoreType.DMA((2,)),
        ],
        compiler_params=pltpu.CompilerParams(collective_id=0, has_side_effects=True),
    )(local)


def pack_kernel(
    sizes, dims, short, win_ref, local_ref, sibling_ref, blocks_ref, pack_ref, codes_ref, sem
):
    rows, cols, depths = sizes
    local_rows, panels, slots = dims
    window = rows * depths
    capacity = pack_ref.shape[1]
    r, c, d = position()
    me_q = r * depths + d
    owner = d // panels
    left_panel = d % panels
    counts_at = panels * slots
    limit = jnp.where(owner == c, capacity, short)

    def entry(q, n, row, panel, slot):
        return pltpu.make_async_copy(blocks_ref.at[row, panel, slot], pack_ref.at[q, n], sem)

    def pack_row(q, carry):
        too_long, copies = carry
        left_at = q * cols + owner
        out_at = q * cols + c
        left_count = win_ref[left_at, 0, counts_at + left_panel]
        on_chip = q % depths == d
        limit_q = jnp.where(on_chip, capacity, limit)
        room = jnp.where(q == me_q, 0, limit_q)
        from_back = (r == 1) & jnp.logical_not(on_chip)

        def left_step(a, counts):
            place = win_ref[left_at, 0, left_panel * slots + a]
            row = place % local_rows
            mine = place // local_rows == r

            def matches(inner_ref, found, n):
                def panel_step(panel, n):
                    out_count = win_ref[out_at, 0, counts_at + panel]
                    inner_count = inner_ref[counts_at + panel, row]

                    def inner_step(t, n):
                        column = inner_ref[panel * slots + t, row]

                        def out_step(s, n):
                            hit = win_ref[out_at, 0, panel * slots + s] == column
                            found(hit, n, panel, t, s)
                            return n + hit.astype(jnp.int32)

                        return lax.fori_loop(0, out_count, out_step, n)

                    return lax.fori_loop(0, inner_count, inner_step, n)

                return lax.fori_loop(0, panels, panel_step, n)

            def keep(hit, n, panel, t, s):
                @pl.when(hit)
                def _():
                    codes_ref[q, 0, HEAD + n] = a * counts_at + panel * slots + s
                    codes_ref[q, 0, SOURCE + n] = (row * panels + panel) * slots + t

                @pl.when(hit & (n < room))
                def _():
                    entry(q, jnp.where(from_back, limit - 1 - n, n), row, panel, t).start()

            def skip(hit, n, panel, t, s):
                pass

            n, other = counts
            return lax.cond(
                mine,
                lambda: (matches(local_ref, keep, n), other),
                lambda: (n, matches(sibling_ref, skip, other)),
            )

        zero = jnp.int32(0)
        n, other = lax.fori_loop(0, left_count, left_step, (zero, zero))
        codes_ref[q, 0, 0] = n
        total = jnp.where(on_chip, n, n + other)
        over = ((total > limit_q) & (q != me_q)).astype(jnp.int32)
        return too_long | over, copies + jnp.minimum(n, room)

    zero = jnp.int32(0)
    too_long, copies = lax.fori_loop(0, window, pack_row, (zero, zero))

    @pl.loop(0, window)
    def _(q):
        codes_ref[q, 0, 1] = too_long

    @pl.loop(0, copies)
    def _(n):
        entry(0, 0, 0, 0, 0).wait()


def pack_lists(win, local, sibling, blocks, sizes, short, capacity):
    local_rows, panels, slots, size, _ = blocks.shape
    window = sizes[0] * sizes[2]
    smem = pl.BlockSpec(memory_space=pltpu.SMEM)
    return pl.pallas_call(
        functools.partial(pack_kernel, sizes, (local_rows, panels, slots), short),
        out_shape=(
            jax.ShapeDtypeStruct((window, capacity, size, size), jnp.float32),
            jax.ShapeDtypeStruct((window, 1, LANES), jnp.int32),
        ),
        in_specs=[smem, smem, smem, pl.BlockSpec(memory_space=pltpu.HBM)],
        out_specs=(pl.BlockSpec(memory_space=pltpu.VMEM), smem),
        scratch_shapes=[pltpu.SemaphoreType.DMA],
        compiler_params=pltpu.CompilerParams(vmem_limit_bytes=VMEM_LIMIT),
    )(win, local, sibling, blocks)


def exchange_kernel(
    sizes, panels, short, pack_ref, codes_ref, blocks_ref,
    got_ref, got_codes_ref, lefts_ref,
    merged_ref, code_send, code_recv, left_send, left_recv,
    swap_send, swap_recv, list_send, list_recv, relay_ref, relay_send, relay_recv, own_sem,
):
    rows, cols, depths = sizes
    window = rows * depths
    capacity = pack_ref.shape[1]
    left_ref = blocks_ref.at[0]
    r, c, d = position()
    me = r * depths + d
    diag = d // panels == c
    parts = [(0, short, 0)]
    extra = capacity - short
    ways = [1, 2] if cols == 4 and extra >= 4 else []
    straight = extra // 4 if ways else extra
    if extra:
        parts.append((short, straight, 0))
    if ways:
        parts.append((short + straight, straight, 1))
        parts.append((short + 2 * straight, extra - 2 * straight, 2))

    barrier = pltpu.get_barrier_semaphore()

    @pl.loop(1, window)
    def _(off):
        q = (me + off) % window
        pl.semaphore_signal(barrier, inc=1, device_id=(q // depths, c, q % depths), device_id_type=MESH)

    @pl.loop(1, cols)
    def _(off):
        pl.semaphore_signal(barrier, inc=1, device_id=(r, (c + off) % cols, d), device_id_type=MESH)

    for way in ways:
        @pl.loop(1, depths)
        def _(off):
            device = (r, c ^ way, (d + off) % depths)
            pl.semaphore_signal(barrier, inc=1, device_id=device, device_id_type=MESH)

    own = [
        pltpu.make_async_copy(codes_ref.at[me], got_codes_ref.at[me], own_sem.at[0]),
        pltpu.make_async_copy(left_ref, lefts_ref.at[c], own_sem.at[1]),
    ]
    for copy in own:
        copy.start()
    pl.semaphore_wait(barrier, window - 1 + cols - 1 + len(ways) * (depths - 1))

    def remote(src, dst, send, recv, device):
        return pltpu.make_async_remote_copy(
            src_ref=src, dst_ref=dst, send_sem=send, recv_sem=recv,
            device_id=device, device_id_type=MESH,
        )

    begin, pass_on, end = spread(
        cols, blocks_ref.shape[2], left_ref, lefts_ref, left_send, left_recv
    )

    def code_copy(slot, other):
        return remote(
            codes_ref.at[other], got_codes_ref.at[slot], code_send.at[other], code_recv.at[slot],
            (other // depths, c, other % depths),
        )

    def swap_copy(part, depth):
        first, length, way = parts[part]
        there = pl.ds(first, length)
        return remote(
            pack_ref.at[(1 - r) * depths + depth, there], merged_ref.at[depth, there],
            swap_send.at[part, depth], swap_recv.at[part, depth], (1 - r, c, d),
        )

    def chip_copy():
        return remote(
            pack_ref.at[(1 - r) * depths + d], got_ref.at[d],
            swap_send.at[0, d], swap_recv.at[0, d], (1 - r, c, d),
        )

    def list_copy(part, slot, depth):
        first, length, way = parts[part]
        there = pl.ds(first, length)
        if way:
            target, device = relay_ref.at[way - 1, depth, pl.ds(0, length)], (r, c ^ way, d)
        else:
            target, device = got_ref.at[slot, there], (r, c, depth)
        return remote(
            merged_ref.at[depth, there], target,
            list_send.at[part, depth], list_recv.at[part, depth if way else slot], device,
        )

    def relay_copy(part, slot, depth):
        first, length, way = parts[part]
        return remote(
            relay_ref.at[way - 1, depth, pl.ds(0, length)],
            got_ref.at[slot, pl.ds(first, length)],
            relay_send.at[part, depth], relay_recv.at[part, slot], (r, c ^ way, depth),
        )

    def arrival(part, depth):
        copy = relay_copy if parts[part][2] else list_copy
        return copy(part, depth, depth)

    def each_part(wide, action):
        if len(parts) > 1:
            @pl.when(wide)
            def _():
                for part in reversed(range(1, len(parts))):
                    action(part)
        action(0)

    def each_relay(action):
        for part, (first, length, way) in enumerate(parts):
            if way:
                @pl.when(d // panels == c ^ way)
                def _():
                    @pl.loop(1, depths)
                    def _(off):
                        action(part, (d + off) % depths)

    @pl.loop(1, depths)
    def _(off):
        depth = (d + off) % depths
        each_part(diag, lambda part: swap_copy(part, depth).start())

    @pl.loop(1, depths)
    def _(off):
        depth = (d + off) % depths

        def forward(part):
            swap_copy(part, depth).wait_recv()
            first, length, way = parts[part]
            q = r * depths + depth
            count = jnp.broadcast_to(codes_ref[q, 0:1, 0:1], pack_ref.shape[2:])
            for place in range(first, first + length):
                rank = jnp.where(r == 1, jnp.where(diag, capacity, short) - 1 - place, place)
                merged_ref[depth, place] = jnp.where(
                    rank < count, pack_ref[q, place], merged_ref[depth, place]
                )
            list_copy(part, d, depth).start()

        each_part(diag, forward)

    begin()
    chip_copy().start()

    @pl.loop(1, window)
    def _(off):
        code_copy(me, (me + off) % window).start()

    def relay(part, depth):
        list_copy(part, d, depth).wait_recv()
        relay_copy(part, d, depth).start()

    each_relay(relay)

    for copy in own:
        copy.wait()

    pass_on()
    end()

    @pl.loop(1, window)
    def _(off):
        other = (me + off) % window
        code_copy(other, other).wait_recv()
        code_copy(me, other).wait_send()

    chip_copy().wait()

    @pl.loop(1, depths)
    def _(off):
        depth = (d + off) % depths
        each_part(diag, lambda part: swap_copy(part, depth).wait_send())
        each_part(depth // panels == c, lambda part: arrival(part, depth).wait_recv())
        each_part(diag, lambda part: list_copy(part, d, depth).wait_send())

    each_relay(lambda part, depth: relay_copy(part, d, depth).wait_send())


def exchange(pack, codes, blocks, sizes, short, ident):
    window, capacity, size, _ = pack.shape
    rows, cols, depths = sizes
    panels = blocks.shape[1]
    vmem = pl.BlockSpec(memory_space=pltpu.VMEM)
    lists = (depths, capacity, size, size)
    sem = pltpu.SemaphoreType.DMA
    return pl.pallas_call(
        functools.partial(exchange_kernel, sizes, panels, short),
        out_shape=(
            jax.ShapeDtypeStruct(lists, jnp.float32),
            jax.ShapeDtypeStruct(codes.shape, jnp.int32),
            jax.ShapeDtypeStruct((cols,) + blocks.shape[1:], jnp.float32),
        ),
        in_specs=[vmem, vmem, pl.BlockSpec(memory_space=pltpu.HBM)],
        out_specs=(vmem,) * 3,
        scratch_shapes=[
            pltpu.VMEM(lists, jnp.float32),
            sem((window,)), sem((window,)), sem((2, max(3, cols))), sem((2, cols)),
            sem((4, depths)), sem((4, depths)), sem((4, depths)), sem((4, depths)),
            pltpu.VMEM((2, depths, max(1, (capacity - short) // 2), size, size), jnp.float32),
            sem((4, depths)), sem((4, depths)), sem((2,)),
        ],
        compiler_params=pltpu.CompilerParams(
            collective_id=ident, has_side_effects=True, vmem_limit_bytes=VMEM_LIMIT
        ),
    )(pack, codes, blocks)


def halves(value):
    high = value.astype(jnp.bfloat16)
    return high, (value - high.astype(jnp.float32)).astype(jnp.bfloat16)


def product(left, right):
    left_high, left_low = halves(left)
    right_high, right_low = halves(right)
    dot = functools.partial(jnp.dot, preferred_element_type=jnp.float32)
    return dot(left_high, right_high) + (dot(left_high, right_low) + dot(left_low, right_high))


def multiply_into(acc_ref, lefts_ref, got_ref, blocks_ref, codes_ref, held, sems, sizes, short):
    rows, cols, depths = sizes
    window = rows * depths
    capacity = got_ref.shape[1]
    panels, slots = blocks_ref.shape[1:3]
    out_slots = panels * slots
    r, c, d = position()
    me_q = r * depths + d
    own = codes_ref[me_q, 0, 0]

    def fetch(n):
        at = codes_ref[me_q, 0, SOURCE + n]
        row = at // out_slots
        block = blocks_ref.at[row, (at // slots) % panels, at % slots]
        return pltpu.make_async_copy(block, held.at[n], sems.at[n])

    @pl.loop(0, own)
    def _(n):
        fetch(n).start()

    acc_ref[...] = jnp.zeros_like(acc_ref)

    def add(q, n, right):
        code = codes_ref[q, 0, HEAD + n]
        depth = q % depths
        left = lefts_ref[depth // panels, depth % panels, code // out_slots]
        s = code % out_slots
        acc_ref[s // slots, s % slots] += product(left, right)

    @pl.loop(0, window)
    def _(q):
        depth = q % depths
        on_chip = depth == d
        room = jnp.where(on_chip | (depth // panels == c), capacity, short)
        from_back = (q // depths == 1) & jnp.logical_not(on_chip)
        count = jnp.where(q == me_q, 0, jnp.minimum(codes_ref[q, 0, 0], room))

        @pl.loop(0, count)
        def _(n):
            add(q, n, got_ref[depth, jnp.where(from_back, room - 1 - n, n)])

    @pl.loop(0, own)
    def _(n):
        fetch(n).wait()
        add(me_q, n, held[n])


def square_kernel(
    sizes, short, codes_ref, got_ref, blocks_ref, lefts_ref, out_ref, held, sems
):
    multiply_into(out_ref, lefts_ref, got_ref, blocks_ref, codes_ref, held, sems, sizes, short)


def cube_kernel(
    sizes, short, codes_ref, got_ref, blocks_ref, lefts_ref, square_ref, out_ref, held, sems
):
    multiply_into(out_ref, lefts_ref, got_ref, blocks_ref, codes_ref, held, sems, sizes, short)
    out_ref[...] = 3.0 * square_ref[...] - 2.0 * out_ref[...]


def local_product(kernel, codes, got, blocks, lefts, extra, out_shape, out_specs):
    vmem = pl.BlockSpec(memory_space=pltpu.VMEM)
    _, panels, slots, size, _ = blocks.shape
    most = slots * slots * panels
    return pl.pallas_call(
        kernel,
        out_shape=out_shape,
        in_specs=[
            pl.BlockSpec(memory_space=pltpu.SMEM),
            vmem,
            pl.BlockSpec(memory_space=pltpu.HBM),
            vmem,
        ] + [vmem] * len(extra),
        out_specs=out_specs,
        scratch_shapes=[
            pltpu.VMEM((most, size, size), jnp.float32),
            pltpu.SemaphoreType.DMA((most,)),
        ],
        compiler_params=pltpu.CompilerParams(vmem_limit_bytes=VMEM_LIMIT),
    )(codes, got, blocks, lefts, *extra)


def gather_kernel(
    cols, square_ref, codes_ref, squares_ref, any_ref, flag_ref, flags_ref,
    send_sem, recv_sem, flag_send, flag_recv, own_sem,
):
    r, c, d = position()
    barrier = pltpu.get_barrier_semaphore()

    @pl.loop(1, cols)
    def _(off):
        pl.semaphore_signal(barrier, inc=1, device_id=(r, (c + off) % cols, d), device_id_type=MESH)

    flag_ref[...] = jnp.max(codes_ref[...], axis=0)
    own = [
        pltpu.make_async_copy(square_ref, squares_ref.at[c], own_sem.at[0]),
        pltpu.make_async_copy(flag_ref, flags_ref.at[c], own_sem.at[1]),
    ]
    for copy in own:
        copy.start()
    begin, pass_on, end = spread(
        cols, square_ref.shape[1], square_ref, squares_ref, send_sem, recv_sem
    )
    pl.semaphore_wait(barrier, cols - 1)

    def flag_copy(slot, other):
        return pltpu.make_async_remote_copy(
            src_ref=flag_ref,
            dst_ref=flags_ref.at[slot],
            send_sem=flag_send.at[other],
            recv_sem=flag_recv.at[slot],
            device_id=(r, other, d),
            device_id_type=MESH,
        )

    begin()

    @pl.loop(1, cols)
    def _(off):
        flag_copy(c, (c + off) % cols).start()

    pass_on()
    for copy in own:
        copy.wait()

    @pl.loop(1, cols)
    def _(off):
        other = (c + off) % cols
        flag_copy(other, other).wait_recv()
        flag_copy(c, other).wait_send()

    end()
    any_ref[...] = jnp.max(flags_ref[...], axis=0)


def gather_square(square, codes, cols, ident):
    vmem = pl.BlockSpec(memory_space=pltpu.VMEM)
    return pl.pallas_call(
        functools.partial(gather_kernel, cols),
        out_shape=(
            jax.ShapeDtypeStruct((cols,) + square.shape, jnp.float32),
            jax.ShapeDtypeStruct(codes.shape[1:], jnp.int32),
        ),
        in_specs=[vmem] * 2,
        out_specs=(vmem,) * 2,
        scratch_shapes=[
            pltpu.VMEM(codes.shape[1:], jnp.int32),
            pltpu.VMEM((cols,) + codes.shape[1:], jnp.int32),
            pltpu.SemaphoreType.DMA((2, max(3, cols))),
            pltpu.SemaphoreType.DMA((2, cols)),
            pltpu.SemaphoreType.DMA((cols,)),
            pltpu.SemaphoreType.DMA((cols,)),
            pltpu.SemaphoreType.DMA((2,)),
        ],
        compiler_params=pltpu.CompilerParams(collective_id=ident, has_side_effects=True),
    )(square, codes)


def body(sizes, blocks, columns, counts):
    rows, cols, depths = sizes
    local_rows, panels, slots, size, _ = blocks.shape
    most = slots * slots * panels
    local = jnp.concatenate([columns.reshape(local_rows, panels * slots).T, counts.T], 0)
    entries = local.shape[0]
    local = jnp.pad(local, ((0, -entries % 8), (0, -local_rows % LANES)))
    win, sibling = gather_meta(local, sizes, panels, entries)
    block_shape = jax.ShapeDtypeStruct(blocks.shape[1:], jnp.float32)
    vmem = pl.BlockSpec(memory_space=pltpu.VMEM)

    def square_step(short, capacity, ident):
        pack, codes = pack_lists(win, local, sibling, blocks, sizes, short, capacity)
        got, got_codes, lefts = exchange(pack, codes, blocks, sizes, short, ident)
        square = local_product(
            functools.partial(square_kernel, sizes, short),
            got_codes, got, blocks, lefts, (), block_shape, vmem,
        )
        squares, too_long = gather_square(square, got_codes, cols, ident + 1)
        return got, got_codes, square, squares, too_long

    def cube_step(short, got, got_codes, square, squares):
        return local_product(
            functools.partial(cube_kernel, sizes, short),
            got_codes, got, blocks, squares, (square,), block_shape, vmem,
        )

    sizes_tried = []
    for short, capacity in TIERS:
        tier = (min(short, most), min(capacity, most))
        if tier not in sizes_tried:
            sizes_tried.append(tier)
    sizes_tried.append((most, most))

    def attempt(tier):
        short, capacity = sizes_tried[tier]
        *lists, too_long = square_step(short, capacity, 1 + 2 * tier)
        if (short, capacity) == (most, most):
            return cube_step(short, *lists)
        return lax.cond(
            too_long[0, 1] != 0, lambda: attempt(tier + 1), lambda: cube_step(short, *lists)
        )

    out = attempt(0)
    return out[None]


def solution(mesh):
    placed = (
        P(("row", "depth"), "col", None, None, None),
        P(("row", "depth"), "col", None),
        P(("row", "depth"), "col"),
    )
    sizes = (mesh.shape["row"], mesh.shape["col"], mesh.shape["depth"])
    return jax.shard_map(
        functools.partial(body, sizes),
        mesh=mesh,
        in_specs=placed,
        out_specs=P(("row", "depth"), "col", None, None, None),
        check_vma=False,
    )
```

profile of v0, /device:TPU:0, one launch (start us, length us, event | category | flops | bytes accessed | tf_op | source)
XLA Modules:
  0.0 62.3 jit_solution(1338640313142871850)
XLA Ops:
  0.0 0.7 %pad_add_fusion = s32[5,64]{1,0:T(8,128)S(1)} fusion(s32[1,64]{1,0:T(1,128)} %bitcast.10, s32[4,64]{1,0:T(4,128)} %bitcast.9), kind=kLoop, calls=%fused_computation | loop fusion | flops 320 | bytes 2560 | tf_op jit(solution)/shard_map/concatenate | solution.py:699
  0.7 9.7 %shard_map.39 = (s32[32,1,128]{2,1,0:T(1,128)S(1)}, s32[8,128]{1,0:T(8,128)S(1)}) custom-call(s32[8,128]{1,0:T(8,128)S(1)} %pad.4.local_ref), custom_call_target="tpu_custom_call" | custom-call | tf_op jit(solution)/shard_map/pallas_call | solution.py:191
  10.4 5.8 %shard_map.40 = (f32[8,6,128,128]{3,2,1,0:T(8,128)S(1)}, s32[8,1,128]{2,1,0:T(1,128)S(1)}) custom-call(s32[32,1,128]{2,1,0:T(1,128)S(1)} %get-tuple-element.89.win_ref, s32[8,128]{1,0:T(8,128)S(1)} %pad.4.local_ref, s32[8,128]{1,0:T(8,128)S(1)} %get-tuple-element.90.sibling_ref, f32[64,1,4,128,128]{4,3,2,1,0:T(8,128)} %blocks_ref.5), custom_call_target="tpu_custom_call" | custom-call | tf_op jit(solution)/shard_map/pallas_call | solution.py:304
  16.3 24.4 %shard_map.41 = (f32[4,6,128,128]{3,2,1,0:T(8,128)S(1)}, s32[8,1,128]{2,1,0:T(1,128)S(1)}, f32[4,1,4,128,128]{4,3,2,1,0:T(8,128)S(1)}) custom-call(f32[8,6,128,128]{3,2,1,0:T(8,128)S(1)} %get-tuple-element.91.pack_ref, s32[8,1,128]{2,1,0:T(1,128)S(1)} %get-tuple-element.92.codes_ref, f32[64,1,4,128,128]{4,3,2,1,0:T(8,128)} %blocks_ref.5), custom_call_target="tpu_custom_call" | custom-call | tf_op jit(solution)/shard_map/pallas_call | solution.py:503
  40.7 2.5 %shard_map.42.square_ref = f32[1,4,128,128]{3,2,1,0:T(8,128)S(1)} custom-call(s32[8,1,128]{2,1,0:T(1,128)S(1)} %get-tuple-element.93.codes_ref, f32[4,6,128,128]{3,2,1,0:T(8,128)S(1)} %get-tuple-element.94.got_ref, f32[64,1,4,128,128]{4,3,2,1,0:T(8,128)} %blocks_ref.5, f32[4,1,4,128,128]{4,3,2,1,0:T(8,128)S(1)} %get-tuple-element.95.lefts_ref), custom_call_target="tpu_custom_call" | custom-call | tf_op jit(solution)/shard_map/pallas_call | solution.py:601
  43.2 14.1 %shard_map.43 = (f32[4,1,4,128,128]{4,3,2,1,0:T(8,128)S(1)}, s32[1,128]{1,0:T(1,128)}) custom-call(f32[1,4,128,128]{3,2,1,0:T(8,128)S(1)} %shard_map.42.square_ref, s32[8,1,128]{2,1,0:T(1,128)S(1)} %get-tuple-element.93.codes_ref), custom_call_target="tpu_custom_call" | custom-call | tf_op jit(solution)/shard_map/pallas_call | solution.py:674
  57.2 1.2 %slice.6 = s32[1,1]{1,0:T(1,128)} slice(s32[1,128]{1,0:T(1,128)} %get-tuple-element.96), slice={[0:1], [1:2]} | slice | bytes 8 | tf_op jit(solution)/shard_map/slice | solution.py:735
  59.1 3.2 %conditional.2 = ((f32[1,1,4,128,128]{4,3,2,1,0:T(8,128)})) conditional(s32[]{:T(128)} %bitcast.7, (s32[8,1,128]{2,1,0:T(1,128)S(1)}, f32[4,6,128,128]{3,2,1,0:T(8,128)S(1)}, f32[64,1,4,128,128]{4,3,2,1,0:T(8,128)}, f32[4,1,4,128,128]{4,3,2,1,0:T(8,128)S(1)}, f32[1,4,128,128]{3,2,1,0:T(8,128)S(1)}) %tuple.18, (s32[32,1,128]{2,1,0:T(1,128)S(1)}, ...), branch_computations={%region_0.1_spmd, %region_1.4_spmd} | conditional | flops 2 | bytes 39878928 | solution.py:734
  59.1 3.2 %branch_0_fun.2 = f32[1,4,128,128]{3,2,1,0:T(8,128)} custom-call(s32[8,1,128]{2,1,0:T(1,128)S(1)} %get-tuple-element.49.codes_ref, f32[4,6,128,128]{3,2,1,0:T(8,128)S(1)} %get-tuple-element.50.got_ref, f32[64,1,4,128,128]{4,3,2,1,0:T(8,128)} %get-tuple-element.51.blocks_ref, f32[4,1,4,128,128]{4,3,2,1,0:T(8,128)S(1)} %get-tuple-element.52.lefts_ref, ...), custom_call_target="tpu_custom_call" | custom-call | tf_op jit(solution)/shard_map/cond/branch_0_fun/pallas_call | solution.py:601
  (1 shorter events, 0.0 us)
where the time goes:
time: 62.2 us; the launch traced here: 62.3 us
  Pallas kernels  59.7 us (96%)
  local copies, waits for them, and re-layouts  1.2 us (2%)
  other arithmetic  0.71 us (1%)
  between operations  0.7 us (1%)
    pallas_call x1, Pallas kernels, exchange(): pl.pallas_call(functools.partial(exchange_kernel, sizes, panels, short),...  24.4 us
    pallas_call x1, Pallas kernels, gather_square(): pl.pallas_call(functools.partial(gather_kernel, cols), out_shape=(jax.Sha...  14.1 us
    pallas_call x1, Pallas kernels, gather_meta(): pl.pallas_call(functools.partial(meta_kernel, sizes, panels, entries), ou...  9.71 us
    pallas_call x1, Pallas kernels, pack_lists(): pl.pallas_call(functools.partial(pack_kernel, sizes, (local_rows, panels,...  5.84 us
    pallas_call x2, Pallas kernels, local_product(): pl.pallas_call(kernel, out_shape=out_shape, in_specs=[pl.BlockSpec(memory...  5.68 us

commit v1 on v0

--- a/solution.py
+++ b/solution.py
@@ -666,7 +666,8 @@
         flag_copy(c, other).wait_send()
 
     end()
-    any_ref[...] = jnp.max(flags_ref[...], axis=0)
+    flags = jnp.max(flags_ref[...], axis=0)
+    any_ref[...] = jnp.broadcast_to(flags[:, 1:2], flags.shape)
 
 
 def gather_square(square, codes, cols, ident):
@@ -732,7 +733,7 @@
         if (short, capacity) == (most, most):
             return cube_step(short, *lists)
         return lax.cond(
-            too_long[0, 1] != 0, lambda: attempt(tier + 1), lambda: cube_step(short, *lists)
+            too_long[0, 0] != 0, lambda: attempt(tier + 1), lambda: cube_step(short, *lists)
         )
 
     out = attempt(0)

time: 62.2 us -> 61.1 us (0.982); the launches traced: 62.3 us -> 60.4 us
  local copies, waits for them, and re-layouts: 1.2 us -> 0.01 us
  Pallas kernels: 59.7 us -> 59 us
    pallas_call x2, Pallas kernels: 5.68 us -> 4.31 us  [local_product(): pl.pallas_call(kernel, out_shape=out_shape, in_specs=[pl.BlockSpec(memory...]
    slice x1 -> x0, local copies, waits for them, and re-layouts: 1.19 us -> none  [attempt(): too_long[0, 1] != 0]
    pallas_call x1, Pallas kernels: 5.84 us -> 6.65 us  [pack_lists(): pl.pallas_call(functools.partial(pack_kernel, sizes, (local_rows, panels,...]
where the time goes in v1:
time: 61.1 us; the launch traced here: 60.4 us
  Pallas kernels  59 us (97%)
  other arithmetic  0.71 us (1%)
  between operations  0.67 us (1%)
    pallas_call x1, Pallas kernels, exchange(): pl.pallas_call(functools.partial(exchange_kernel, sizes, panels, short),...  24.3 us
    pallas_call x1, Pallas kernels, gather_square(): pl.pallas_call(functools.partial(gather_kernel, cols), out_shape=(jax.Sha...  14.1 us
    pallas_call x1, Pallas kernels, gather_meta(): pl.pallas_call(functools.partial(meta_kernel, sizes, panels, entries), ou...  9.71 us
    pallas_call x1, Pallas kernels, pack_lists(): pl.pallas_call(functools.partial(pack_kernel, sizes, (local_rows, panels,...  6.65 us
    pallas_call x2, Pallas kernels, local_product(): pl.pallas_call(kernel, out_shape=out_shape, in_specs=[pl.BlockSpec(memory...  4.31 us

profile of v1, /device:TPU:0, one launch (start us, length us, event | category | flops | bytes accessed | tf_op | source)
XLA Modules:
  0.0 60.4 jit_solution(11545884263597595743)
XLA Ops:
  0.0 0.7 %pad_add_fusion = s32[5,64]{1,0:T(8,128)S(1)} fusion(s32[1,64]{1,0:T(1,128)} %bitcast.12, s32[4,64]{1,0:T(4,128)} %bitcast.11), kind=kLoop, calls=%fused_computation | loop fusion | flops 320 | bytes 2560 | tf_op jit(solution)/shard_map/concatenate | solution.py:700
  0.7 9.7 %shard_map.39 = (s32[32,1,128]{2,1,0:T(1,128)S(1)}, s32[8,128]{1,0:T(8,128)S(1)}) custom-call(s32[8,128]{1,0:T(8,128)S(1)} %pad.4.local_ref), custom_call_target="tpu_custom_call" | custom-call | tf_op jit(solution)/shard_map/pallas_call | solution.py:191
  10.4 6.7 %shard_map.40 = (f32[8,6,128,128]{3,2,1,0:T(8,128)S(1)}, s32[8,1,128]{2,1,0:T(1,128)S(1)}) custom-call(s32[32,1,128]{2,1,0:T(1,128)S(1)} %get-tuple-element.89.win_ref, s32[8,128]{1,0:T(8,128)S(1)} %pad.4.local_ref, s32[8,128]{1,0:T(8,128)S(1)} %get-tuple-element.90.sibling_ref, f32[64,1,4,128,128]{4,3,2,1,0:T(8,128)} %blocks_ref.5), custom_call_target="tpu_custom_call" | custom-call | tf_op jit(solution)/shard_map/pallas_call | solution.py:304
  17.1 24.3 %shard_map.41 = (f32[4,6,128,128]{3,2,1,0:T(8,128)S(1)}, s32[8,1,128]{2,1,0:T(1,128)S(1)}, f32[4,1,4,128,128]{4,3,2,1,0:T(8,128)S(1)}) custom-call(f32[8,6,128,128]{3,2,1,0:T(8,128)S(1)} %get-tuple-element.91.pack_ref, s32[8,1,128]{2,1,0:T(1,128)S(1)} %get-tuple-element.92.codes_ref, f32[64,1,4,128,128]{4,3,2,1,0:T(8,128)} %blocks_ref.5), custom_call_target="tpu_custom_call" | custom-call | tf_op jit(solution)/shard_map/pallas_call | solution.py:503
  41.4 1.8 %shard_map.42.square_ref = f32[1,4,128,128]{3,2,1,0:T(8,128)S(1)} custom-call(s32[8,1,128]{2,1,0:T(1,128)S(1)} %get-tuple-element.93.codes_ref, f32[4,6,128,128]{3,2,1,0:T(8,128)S(1)} %get-tuple-element.94.got_ref, f32[64,1,4,128,128]{4,3,2,1,0:T(8,128)} %blocks_ref.5, f32[4,1,4,128,128]{4,3,2,1,0:T(8,128)S(1)} %get-tuple-element.95.lefts_ref), custom_call_target="tpu_custom_call" | custom-call | tf_op jit(solution)/shard_map/pallas_call | solution.py:601
  43.2 14.1 %shard_map.43 = (f32[4,1,4,128,128]{4,3,2,1,0:T(8,128)S(1)}, s32[1,128]{1,0:T(1,128)}) custom-call(f32[1,4,128,128]{3,2,1,0:T(8,128)S(1)} %shard_map.42.square_ref, s32[8,1,128]{2,1,0:T(1,128)S(1)} %get-tuple-element.93.codes_ref), custom_call_target="tpu_custom_call" | custom-call | tf_op jit(solution)/shard_map/pallas_call | solution.py:675
  57.9 2.5 %conditional.2 = ((f32[1,1,4,128,128]{4,3,2,1,0:T(8,128)})) conditional(s32[]{:T(128)} %bitcast.7, (s32[8,1,128]{2,1,0:T(1,128)S(1)}, f32[4,6,128,128]{3,2,1,0:T(8,128)S(1)}, f32[64,1,4,128,128]{4,3,2,1,0:T(8,128)}, f32[4,1,4,128,128]{4,3,2,1,0:T(8,128)S(1)}, f32[1,4,128,128]{3,2,1,0:T(8,128)S(1)}) %tuple.18, (s32[32,1,128]{2,1,0:T(1,128)S(1)}, ...), branch_computations={%region_0.1_spmd, %region_1.4_spmd} | conditional | flops 2 | bytes 39878920 | solution.py:735
  57.9 2.5 %branch_0_fun.2 = f32[1,4,128,128]{3,2,1,0:T(8,128)} custom-call(s32[8,1,128]{2,1,0:T(1,128)S(1)} %get-tuple-element.49.codes_ref, f32[4,6,128,128]{3,2,1,0:T(8,128)S(1)} %get-tuple-element.50.got_ref, f32[64,1,4,128,128]{4,3,2,1,0:T(8,128)} %get-tuple-element.51.blocks_ref, f32[4,1,4,128,128]{4,3,2,1,0:T(8,128)S(1)} %get-tuple-element.52.lefts_ref, ...), custom_call_target="tpu_custom_call" | custom-call | tf_op jit(solution)/shard_map/cond/branch_0_fun/pallas_call | solution.py:601
  (1 shorter events, 0.0 us)
